TPU v7x, 256 devices: a whole 4x4x8 slice. The times are simulated.
256 devices in a mesh: tok: 16 (over x, z_hi, core), ch: 16 (over y, z_lo).
Axes of the slice: x: 4, y: 4, z: 8 (z_hi: 2, z_lo: 4; z = z_hi * 4 + z_lo), core: 2. Of those that a mesh axis runs over, the one named last changes fastest.
Arguments:
- tokens: bfloat16 [6144, 8192], P('tok', 'ch'), may hold values from -6 to 6
- value_weight: bfloat16 [8192, 8192], P('tok', 'ch'), may hold values from -0.0625 to 0.0625
- key_gate: bfloat16 [6144, 8192], P('tok', 'ch'), may hold values from -6 to 6
- query_gate: bfloat16 [6144, 8192], P('tok', 'ch'), may hold values from -6 to 6
- conv_filter: float32 [512, 128], P('ch'), may hold values from -0.5 to 0.5
- out_weight: bfloat16 [8192, 8192], P('tok', 'ch'), may hold values from -0.0625 to 0.0625
Outputs:
- mixed: bfloat16 [6144, 8192], P('tok', 'ch')
All inputs are finite; a program needn't handle non-finite values.
Results may differ from a plain program's by a relative error of at most 0.02.
Values may be sent and summed in bfloat16 or wider, within the bound.
A program may use at most 64 MiB of HBM per device.

v0:
```python
import jax
import jax.numpy as jnp
from jax import lax
from jax.sharding import PartitionSpec as P

TAPS = 128
GROUP = 16


def passed_along(block, axis, distance):
    devices = range(lax.axis_size(axis))
    route = [(i - distance, i) for i in devices if i - distance in devices]
    return lax.ppermute(block, axis, route)


def banded_blocks(conv_filter):
    groups_dev = conv_filter.shape[0]
    span = conv_filter.shape[1]
    period = 3 * span
    first = jnp.zeros((groups_dev, 1), jnp.float32)
    trailing = jnp.zeros((groups_dev, 2 * span - 1), jnp.float32)
    pattern = jnp.concatenate([first, conv_filter[:, ::-1], trailing], axis=1)
    tiled = jnp.tile(pattern, (1, span))
    shaped_rows = tiled[:, : span * (period - 1)].reshape(groups_dev, span, period - 1)
    return shaped_rows[:, :, : 2 * span]


def on_device(tokens, value_weight, key_gate, query_gate, conv_filter, out_weight):
    tok_rows = tokens.shape[0]
    width_dev = value_weight.shape[1]
    gathered = lax.all_gather(tokens, "ch", axis=1, tiled=True)
    columns = gathered
    values = jnp.dot(
        columns,
        lax.all_gather(value_weight, "tok", axis=0, tiled=True),
        preferred_element_type=jnp.float32,
    )
    values = values.astype(jnp.bfloat16)
    gated = (values.astype(jnp.float32) * key_gate.astype(jnp.float32)).astype(jnp.bfloat16)
    rim_rows = passed_along(gated[tok_rows - (TAPS - 1) :], "tok", 1)
    groups_dev = conv_filter.shape[0]
    leading = jnp.zeros((1, width_dev), jnp.bfloat16)
    extended = jnp.concatenate([leading, rim_rows, gated], axis=0)
    blocks_dev = tok_rows // TAPS
    stacked = extended.reshape(blocks_dev + 1, TAPS, groups_dev, GROUP)
    paired = jnp.concatenate([stacked[:-1], stacked[1:]], axis=1)
    banded = banded_blocks(conv_filter)
    banded_high = banded.astype(jnp.bfloat16)
    banded_low = (banded - banded_high.astype(jnp.float32)).astype(jnp.bfloat16)
    conv = jnp.einsum("gts,bsgc->btgc", banded_high, paired, preferred_element_type=jnp.float32)
    conv = conv + jnp.einsum(
        "gts,bsgc->btgc", banded_low, paired, preferred_element_type=jnp.float32
    )
    conv = conv.reshape(tok_rows, width_dev)
    shaped = (conv * query_gate.astype(jnp.float32)).astype(jnp.bfloat16)
    shaped_full = lax.all_gather(shaped, "ch", axis=1, tiled=True)
    columns = shaped_full
    mixed = jnp.dot(
        columns,
        lax.all_gather(out_weight, "tok", axis=0, tiled=True),
        preferred_element_type=jnp.float32,
    )
    return mixed.astype(jnp.bfloat16)


def solution(mesh):
    return jax.shard_map(
        on_device,
        mesh=mesh,
        in_specs=(
            P("tok", "ch"),
            P("tok", "ch"),
            P("tok", "ch"),
            P("tok", "ch"),
            P("ch", None),
            P("tok", "ch"),
        ),
        out_specs=P("tok", "ch"),
        check_vma=False,
    )
```

profile of v0, /device:TPU:1, one launch (start us, length us, event | category | flops | bytes accessed | tf_op | source)
XLA Modules:
  0.0 527.8 jit_solution(4946004300896583172)
XLA Ops:
  6.5 0.0 all-gather.5.cloned.1.call-start
  6.5 0.7 all-gather.5.cloned.1.call-update
  7.3 0.0 all-gather.7.cloned.1.call-start
  7.3 0.7 all-gather.7.cloned.1.call-update
  8.0 0.0 all-gather.11.cloned.1.call-start
  8.1 0.7 all-gather.11.cloned.1.call-update
  8.7 0.0 all-gather.9.cloned.1.call-start
  8.8 0.8 rev.3
  9.6 0.1 pad.2.clone
  9.7 146.9 %all-gather.5.cloned.1.call-done = bf16[384,8192]{1,0:T(8,128)(2,1)} async-done(((bf16[384,512]{1,0:T(8,128)(2,1)}), bf16[384,8192]{1,0:T(8,128)(2,1)}) %all-gather.5.cloned.1.call-update) | async-done | bytes 6291472 | tf_op jit(solution)/shard_map/all_gather | solution.py:31
  156.5 109.1 %all-gather.7.cloned.1.call-done = bf16[8192,512]{1,0:T(8,128)(2,1)} async-done(((bf16[512,512]{1,0:T(8,128)(2,1)}), bf16[8192,512]{1,0:T(8,128)(2,1)}) %all-gather.7.cloned.1.call-update) | async-done | bytes 8388624 | tf_op jit(solution)/shard_map/all_gather | solution.py:35
  265.7 8.6 %fusion.13 = bf16[384,512]{1,0:T(8,128)(2,1)S(1)} fusion(bf16[384,8192]{1,0:T(8,128)(2,1)} %all-gather.5.cloned.1.call-done, bf16[8192,512]{1,0:T(8,128)(2,1)} %all-gather.7.cloned.1.call-done, bf16[384,512]{1,0:T(8,128)(2,1)} %param.8), kind=kOutput, calls=%fused_computation.12 | convolution fusion | flops 3222208512 | bytes 15466496 | tf_op jit(solution)/shard_map/dot_general | solution.py:33
  274.3 2.1 collective-permute-start
  276.4 0.1 maximum_maximum_fusion
  276.5 0.4 tile.4
  276.9 3.6 copy.17
  280.5 3.0 slice.27
  283.5 0.0 copy-start.1
  283.5 9.7 %reshape.13 = f32[32,128,383]{2,1,0:T(8,128)} reshape(f32[32,49024]{1,0:T(8,128)} %slice.27) | data formatting | bytes 12550144 | tf_op jit(solution)/shard_map/reshape | solution.py:24
  293.2 0.0 copy-done.1
  293.2 0.2 copy.14
  293.4 0.2 copy.10
  293.7 0.1 slice.22
  293.8 0.0 collective-permute-done
  293.8 0.1 pad_maximum_fusion
  293.9 0.2 copy.9
  294.2 0.1 slice.21
  294.3 0.0 copy-start
  294.3 0.1 copy_dynamic-update-slice_fusion.1
  294.4 0.1 copy_dynamic-update-slice_fusion
  294.5 3.2 fusion.1
  297.7 0.7 copy-done
  298.4 0.8 fusion.8
  299.2 0.4 copy.13
  299.6 0.9 fusion.14
  300.5 0.0 all-gather.9.cloned.1.call-update
  300.5 72.0 %all-gather.11.cloned.1.call-done = bf16[8192,512]{1,0:T(8,128)(2,1)} async-done(((bf16[512,512]{1,0:T(8,128)(2,1)}), bf16[8192,512]{1,0:T(8,128)(2,1)}) %all-gather.11.cloned.1.call-update) | async-done | bytes 8388624 | tf_op jit(solution)/shard_map/all_gather | solution.py:60
  372.5 139.4 %all-gather.9.cloned.1.call-done = bf16[384,8192]{0,1:T(8,128)(2,1)} async-done(((bf16[384,512]{0,1:T(8,128)(2,1)}), bf16[384,8192]{0,1:T(8,128)(2,1)}) %all-gather.9.cloned.1.call-update) | async-done | bytes 6291472 | tf_op jit(solution)/shard_map/all_gather | solution.py:56
  511.9 9.4 %convolution_convert_fusion = bf16[384,512]{1,0:T(8,128)(2,1)} fusion(bf16[384,8192]{0,1:T(8,128)(2,1)} %all-gather.9.cloned.1.call-done, bf16[8192,512]{1,0:T(8,128)(2,1)} %all-gather.11.cloned.1.call-done), kind=kOutput, calls=%fused_computation.8 | convolution fusion | flops 3221422080 | bytes 15073280 | tf_op jit(solution)/shard_map/dot_general | solution.py:58
  (4 shorter events, 0.0 us)
Async XLA Ops:
  6.5 150.0 %all-gather.5.cloned.1.call-start = ((), (), s32[]{:S(2)}) async-start(), calls=%async_computation | async-start | bytes 6684672 | tf_op jit(solution)/shard_map/all_gather | solution.py:31
  7.3 258.4 %all-gather.7.cloned.1.call-start = ((), (), s32[]{:S(2)}) async-start(), calls=%async_computation.1 | async-start | bytes 8912896 | tf_op jit(solution)/shard_map/all_gather | solution.py:35
  8.0 364.5 %all-gather.11.cloned.1.call-start = ((), (), s32[]{:S(2)}) async-start(), calls=%async_computation.3 | async-start | bytes 8912896 | tf_op jit(solution)/shard_map/all_gather | solution.py:60
  8.7 503.2 %all-gather.9.cloned.1.call-start = ((), (), s32[]{:S(2)}) async-start(), calls=%async_computation.2 | async-start | bytes 6684672 | tf_op jit(solution)/shard_map/all_gather | solution.py:56
  274.3 19.5 %collective-permute-start = (bf16[127,512]{1,0:T(8,128)(2,1)S(1)}, bf16[127,512]{1,0:T(8,128)(2,1)S(1)}, u32[]{:S(2)}, u32[]{:S(2)}) collective-permute-start(bf16[127,512]{1,0:T(8,128)(2,1)S(1)} %slice.25), channel_id=1, source_target_pairs={{0,16},{16,32},{32,48},{48,64},{64,80},{80,96},{96,112},{112,128},... | collective-permute-start | bytes 390152 | tf_op jit(solution)/shard_map/ppermute | solution.py:13
  283.5 9.7 %copy-start.1 = (bf16[384,512]{1,0:T(8,128)(2,1)S(1)}, bf16[384,512]{1,0:T(8,128)(2,1)}, u32[]{:S(2)}) copy-start(bf16[384,512]{1,0:T(8,128)(2,1)} %param.9) | copy-start | bytes 1179652
  294.3 4.1 copy-start
Sparse Core Ops, SparseCore 0:
  9.1 147.3 all-gather.4
  159.2 106.4 all-gather.6
  268.3 104.1 all-gather.10
  374.1 137.7 all-gather.8
where the time goes:
time: 528 us
  waiting for transfers between devices  469 us (89%)
  matrix products  22 us (4%)
  local copies, waits for them, and re-layouts  19.8 us (4%)
  between operations  13.3 us (3%)
    all_gather x1, waiting for transfers between devices, on_device(): gathered = lax.all_gather(tokens, 'ch', axis=1, tiled=True)  147 us
    all_gather x1, waiting for transfers between devices, on_device(): shaped_full = lax.all_gather(shaped, 'ch', axis=1, tiled=True)  139 us
    all_gather x1, waiting for transfers between devices, on_device(): lax.all_gather(value_weight, 'tok', axis=0, tiled=True)  109 us
    all_gather x1, waiting for transfers between devices, on_device(): lax.all_gather(out_weight, 'tok', axis=0, tiled=True)  72 us
  transfers between devices with their start and end apart: 5, of which 4 were waited for; matrix products, arithmetic and copies ran while one was open for 6% of the time, Pallas kernels for 0%

commit v1 on v0

v1 whole, which is shorter than its diff:
```python
import functools

import jax
import jax.numpy as jnp
from jax import lax
from jax.experimental import pallas as pl
from jax.experimental.pallas import tpu as pltpu
from jax.sharding import PartitionSpec as P

MESH = pl.DeviceIdType.MESH
TAPS = 128
GROUP = 16
ROWS = 384
WIDTH = 512
RELAY = 16
WHOLE = ((0, 384),)
PARTS = ((128, 256), (0, 128))


class Names:
    def __init__(self):
        self.index = {}

    def __call__(self, name):
        return self.index.setdefault(name, len(self.index))


def place(x, y, z, c):
    return (x * 4 + (z // 4) * 2 + c, y * 4 + lax.rem(z, 4))


def kernel(
    tok_hbm, wv_hbm, key_hbm, query_hbm, filt_ref, wo_hbm,
    out_ref,
    wbuf_v, wbuf_o, tbuf_v, tbuf_o, band, base, ext, key, query,
    acc_away, acc_own, part_out, part_in, send_sem, recv_sem, local_sem,
):
    tok = lax.axis_index("tok")
    ch = lax.axis_index("ch")
    x, zh, c = tok // 4, lax.rem(tok // 2, 2), lax.rem(tok, 2)
    y, zl = ch // 4, lax.rem(ch, 4)
    zl1, zl0 = zl // 2, lax.rem(zl, 2)
    z = zh * 4 + zl
    master = c == zl0
    nm = jnp.logical_not(master)

    def near(zl0_):
        return zh * 4 + zl1 * 2 + zl0_

    xp, xm, x2 = lax.rem(x + 1, 4), lax.rem(x + 3, 4), lax.rem(x + 2, 4)
    yp, ym, y2 = lax.rem(y + 1, 4), lax.rem(y + 3, 4), lax.rem(y + 2, 4)
    dev_xp, dev_xm = place(xp, y, z, c), place(xm, y, z, c)
    dev_yp, dev_ym = place(x, yp, z, c), place(x, ym, z, c)
    dev_z1 = place(x, y, near(1 - zl0), c)
    dev_z2 = place(x, y, zh * 4 + (1 - zl1) * 2 + zl0, c)
    far_zl0 = jnp.where(master, zl0, 1 - zl0)
    dev_far = place(x, y, (1 - zh) * 4 + zl1 * 2 + far_zl0, jnp.where(master, c, 1 - c))
    dev_sib = place(x, y, z, 1 - c)
    dev_next = (lax.rem(tok + 1, 16), ch)
    dev_prev = (lax.rem(tok + 15, 16), ch)
    dev_other = (jnp.where(c == 1, lax.rem(tok + 1, 16), lax.rem(tok + 15, 16)), ch)

    barrier = pltpu.get_barrier_semaphore()
    partners = (dev_xp, dev_xm, dev_yp, dev_ym, dev_z1, dev_z2, dev_far, dev_sib, dev_other)
    for d in partners:
        pl.semaphore_signal(barrier, inc=1, device_id=d, device_id_type=MESH)
    pl.semaphore_wait(barrier, len(partners))

    w_hbm = (wv_hbm, wo_hbm)
    wbuf = (wbuf_v, wbuf_o)
    tbuf = (tbuf_v, tbuf_o)
    own, away = zl0, 1 - zl0
    names = Names()

    def slot(b, zz, j):
        return b * 8 + zz * 4 + j

    root_z = jnp.where(master, zh, 1 - zh)
    root_b = (jnp.where(master, own, away), jnp.where(master, away, own))

    def copy(name, src, dst, dev):
        i = names(name)
        return pltpu.make_async_remote_copy(
            src_ref=src, dst_ref=dst, send_sem=send_sem.at[i], recv_sem=recv_sem.at[i],
            device_id=dev, device_id_type=MESH,
        )

    def w_in(m, recv=False):
        dst = jnp.where(master, slot(away, zh, x), RELAY) if recv else jnp.where(master, RELAY, slot(own, zh, x))
        return copy(("in", m), w_hbm[m], wbuf[m].at[dst], dev_z1)

    def w_far(m, i, recv=False):
        src = w_hbm[m] if i == 0 else wbuf[m].at[RELAY]
        if recv:
            dst = slot(away if i == 0 else own, 1 - zh, x)
        else:
            dst = slot(own if i == 0 else away, zh, x)
        return copy(("far", m, i), src, wbuf[m].at[dst], dev_far)

    def w_x(m, r, way, recv=False, native=False):
        from_x = (xm if way > 0 else xp) if recv else x
        s = slot(root_b[r], root_z, from_x)
        src = w_hbm[m] if native else wbuf[m].at[s]
        return copy(("x", m, r, way), src, wbuf[m].at[s], dev_xp if way > 0 else dev_xm)

    def w_fwd(m, r, way, recv=False):
        from_x = x2 if recv else (xm if way > 0 else xp)
        rows = pl.ds(0, 256) if way > 0 else pl.ds(256, 256)
        s = wbuf[m].at[slot(root_b[r], root_z, from_x), rows]
        return copy(("fwd", m, r, way), s, s, dev_xp if way > 0 else dev_xm)

    def w_sib(m, r, k, recv=False, native=False):
        j = (x, xm, xp, x2)[k]
        s = slot(1 - root_b[r], 1 - root_z, j) if recv else slot(root_b[r], root_z, j)
        src = w_hbm[m] if native else wbuf[m].at[s]
        return copy(("sib", m, r, k), src, wbuf[m].at[s], dev_sib)

    def t_y(q, ch_, p, way, recv=False):
        first, n = (WHOLE, PARTS)[q][ch_]
        from_y = (ym if way > 0 else yp) if recv else y
        k = (zl1 if p == 0 else 1 - zl1) * 4 + from_y
        ref = tbuf[q].at[k, pl.ds(first, n)]
        src = tok_hbm if q == 0 and p == 0 else ref
        return copy(("ty", q, ch_, p, way), src, ref, dev_yp if way > 0 else dev_ym)

    def t_fwd(q, ch_, p, way, recv=False):
        first, n = (WHOLE, PARTS)[q][ch_]
        from_y = y2 if recv else (ym if way > 0 else yp)
        k = (zl1 if p == 0 else 1 - zl1) * 4 + from_y
        rows = pl.ds(first, n // 2) if way > 0 else pl.ds(first + n // 2, n // 2)
        ref = tbuf[q].at[k, rows]
        return copy(("tfwd", q, ch_, p, way), ref, ref, dev_yp if way > 0 else dev_ym)

    def t_far(q, ch_, recv=False):
        first, n = (WHOLE, PARTS)[q][ch_]
        ref = tbuf[q].at[((1 - zl1) if recv else zl1) * 4 + y, pl.ds(first, n)]
        return copy(("tz", q, ch_), tok_hbm if q == 0 else ref, ref, dev_z2)

    def partial(q, ch_):
        first, n = (WHOLE, PARTS)[q][ch_]
        rows = pl.ds(first, n)
        return copy(("c", q, ch_), part_out.at[q, rows], part_in.at[q, rows], dev_z1)

    def halo():
        return copy(("halo",), ext.at[pl.ds(ROWS, TAPS)], ext.at[pl.ds(0, TAPS)], dev_next)

    def both(make, *a):
        for way in (1, -1):
            make(*a, way).start()

    def relay_x(m, r):
        for way in (1, -1):
            w_x(m, r, way, recv=True).wait_recv()
            w_fwd(m, r, way).start()
        w_sib(m, r, 1).start()
        w_sib(m, r, 2).start()

    def end_x(m, r):
        for way in (1, -1):
            w_fwd(m, r, way, recv=True).wait_recv()
        w_sib(m, r, 3).start()

    def spread(m, r):
        both(w_x, m, r)
        w_sib(m, r, 0).start()

    def relay_y(q, ch_, p):
        for way in (1, -1):
            t_y(q, ch_, p, way, recv=True).wait_recv()
            t_fwd(q, ch_, p, way).start()

    def end_y(q, ch_, p):
        for way in (1, -1):
            t_fwd(q, ch_, p, way, recv=True).wait_recv()

    def first_w(m):
        w_in(m).start()

        @pl.when(nm)
        def _():
            w_far(m, 0).start()

    def native_w(m):
        @pl.when(master)
        def _():
            for way in (1, -1):
                w_x(m, 0, way, native=True).start()
            w_sib(m, 0, 0, native=True).start()

    def inbox_w(m):
        w_in(m, recv=True).wait_recv()

        @pl.when(master)
        def _():
            spread(m, 1)

        @pl.when(nm)
        def _():
            w_far(m, 1).start()

    def root_from_far(m, r):
        @pl.when(nm)
        def _():
            w_far(m, r, recv=True).wait_recv()
            spread(m, r)

    def local(i, src, dst):
        return pltpu.make_async_copy(src, dst, local_sem.at[i])

    def own_w(m):
        return local(m, w_hbm[m], wbuf[m].at[slot(own, zh, x)])

    t_far(0, 0).start()
    first_w(0)
    for way in (1, -1):
        t_y(0, 0, 0, way).start()
    native_w(0)
    own_tok = local(2, tok_hbm, tbuf[0].at[zl1 * 4 + y])
    own_key = local(3, key_hbm, key)
    own_query = local(4, query_hbm, query)
    own_tok.start()
    own_key.start()
    own_query.start()

    @pl.when(master)
    def _():
        own_w(0).start()
        own_w(1).start()

    s_at = lax.broadcasted_iota(jnp.int32, (TAPS, 2 * TAPS), 1)
    j_at = lax.broadcasted_iota(jnp.int32, (TAPS, 2 * TAPS), 0)
    flip = jnp.where(s_at + j_at == TAPS, 1.0, 0.0).astype(jnp.bfloat16)
    base[...] = jnp.dot(filt_ref[...].astype(jnp.bfloat16), flip, preferred_element_type=jnp.float32)

    @pl.loop(0, WIDTH // GROUP)
    def _(g):
        rows = jnp.broadcast_to(base[pl.ds(g, 1), :], (TAPS, 2 * TAPS))
        turned = pltpu.roll(rows, 0, 1, stride=1, stride_axis=0)
        band[pl.ds(pl.multiple_of(g * TAPS, TAPS), TAPS), :] = turned.astype(jnp.bfloat16)

    acc_away[...] = jnp.zeros_like(acc_away)
    acc_own[...] = jnp.zeros_like(acc_own)

    def multiply(q, acc, rows, b, zz):
        @pl.loop(0, 4)
        def _(j):
            lhs = tbuf[q][zz * 4 + j, rows, :]
            w = wbuf[q].at[slot(b, zz, j)]
            for n in range(2):
                cols = pl.ds(n * 256, 256)
                acc[rows, cols] += jnp.dot(lhs, w[:, cols], preferred_element_type=jnp.float32)

    def wait_sib(m, r):
        for k in range(4):
            w_sib(m, r, k, recv=True).wait_recv()

    inbox_w(0)
    relay_y(0, 0, 0)

    @pl.when(master)
    def _():
        relay_x(0, 0)

    root_from_far(0, 0)
    t_far(0, 0, recv=True).wait_recv()
    both(t_y, 0, 0, 1)

    @pl.when(master)
    def _():
        end_x(0, 0)
        relay_x(0, 1)

    @pl.when(nm)
    def _():
        relay_x(0, 0)

    root_from_far(0, 1)
    first_w(1)
    native_w(1)
    relay_y(0, 0, 1)
    end_y(0, 0, 0)

    @pl.when(master)
    def _():
        end_x(0, 1)

    @pl.when(nm)
    def _():
        end_x(0, 0)
        relay_x(0, 1)

    own_tok.wait()
    end_y(0, 0, 1)

    every = pl.ds(0, ROWS)

    @pl.when(master)
    def _():
        own_w(0).wait()
        own_w(1).wait()
        wait_sib(0, 0)

    @pl.when(nm)
    def _():
        wait_sib(0, 1)

    for zz in range(2):
        multiply(0, acc_away, every, away, zz)
    part_out[0] = acc_away[...].astype(jnp.bfloat16)
    partial(0, 0).start()
    inbox_w(1)

    @pl.when(master)
    def _():
        relay_x(1, 0)
        wait_sib(0, 1)

    @pl.when(nm)
    def _():
        end_x(0, 1)
        wait_sib(0, 0)

    for zz in range(2):
        multiply(0, acc_own, every, own, zz)

    root_from_far(1, 0)

    own_key.wait()
    own_query.wait()
    partial(0, 0).wait_recv()
    values = (acc_own[...] + part_in[0].astype(jnp.float32)).astype(jnp.bfloat16)
    ext[pl.ds(TAPS, ROWS), :] = (values.astype(jnp.float32) * key[...].astype(jnp.float32)).astype(jnp.bfloat16)
    halo().start()
    acc_away[...] = jnp.zeros_like(acc_away)
    acc_own[...] = jnp.zeros_like(acc_own)

    lane_group = lax.broadcasted_iota(jnp.int32, (TAPS, TAPS), 1) // GROUP
    k_own = zl1 * 4 + y

    def convolve(block):
        first = block * TAPS
        for tile in range(WIDTH // TAPS):
            lanes = pl.ds(tile * TAPS, TAPS)
            raw = jnp.dot(
                band[pl.ds(tile * 8 * TAPS, 8 * TAPS), :],
                ext[pl.ds(first, 2 * TAPS), lanes],
                preferred_element_type=jnp.float32,
            )
            conv = raw[:TAPS]
            for g in range(1, 8):
                conv = jnp.where(lane_group == g, raw[g * TAPS : (g + 1) * TAPS], conv)
            rows = pl.ds(first, TAPS)
            shaped = conv * query[rows, lanes].astype(jnp.float32)
            tbuf_o[k_own, rows, lanes] = shaped.astype(jnp.bfloat16)

    def send_shaped(ch_):
        t_far(1, ch_).start()
        both(t_y, 1, ch_, 0)

    convolve(1)
    convolve(2)
    send_shaped(0)
    root_from_far(1, 1)
    halo().wait_recv()

    @pl.when(tok == 0)
    def _():
        ext[pl.ds(0, TAPS), :] = jnp.zeros((TAPS, WIDTH), jnp.bfloat16)

    convolve(0)
    send_shaped(1)

    @pl.when(master)
    def _():
        end_x(1, 0)
        relay_x(1, 1)

    relay_y(1, 0, 0)
    t_far(1, 0, recv=True).wait_recv()
    both(t_y, 1, 0, 1)

    @pl.when(nm)
    def _():
        relay_x(1, 0)

    relay_y(1, 1, 0)
    t_far(1, 1, recv=True).wait_recv()
    both(t_y, 1, 1, 1)

    @pl.when(master)
    def _():
        end_x(1, 1)

    @pl.when(nm)
    def _():
        relay_x(1, 1)
        end_x(1, 0)

    relay_y(1, 0, 1)
    end_y(1, 0, 0)

    @pl.when(nm)
    def _():
        end_x(1, 1)

    relay_y(1, 1, 1)
    end_y(1, 0, 1)
    wait_sib(1, 0)
    wait_sib(1, 1)

    for ch_ in range(2):
        rows = pl.ds(*PARTS[ch_])
        if ch_ == 1:
            end_y(1, 1, 0)
            end_y(1, 1, 1)
        for zz in range(2):
            multiply(1, acc_away, rows, away, zz)
        part_out[1, rows] = acc_away[rows].astype(jnp.bfloat16)
        partial(1, ch_).start()
        for zz in range(2):
            multiply(1, acc_own, rows, own, zz)
    for ch_ in range(2):
        rows = pl.ds(*PARTS[ch_])
        partial(1, ch_).wait_recv()
        out_ref[rows] = (acc_own[rows] + part_in[1, rows].astype(jnp.float32)).astype(jnp.bfloat16)

    for m in range(2):
        w_in(m).wait_send()
        for r in range(2):
            for way in (1, -1):
                w_x(m, r, way).wait_send()
                w_fwd(m, r, way).wait_send()
            for k in range(4):
                w_sib(m, r, k).wait_send()

        @pl.when(nm)
        def _():
            w_far(m, 0).wait_send()
            w_far(m, 1).wait_send()

    for q, parts in ((0, WHOLE), (1, PARTS)):
        for ch_ in range(len(parts)):
            for p in range(2):
                for way in (1, -1):
                    t_y(q, ch_, p, way).wait_send()
                    t_fwd(q, ch_, p, way).wait_send()
            t_far(q, ch_).wait_send()
            partial(q, ch_).wait_send()
    halo().wait_send()


COPIES = 96


def on_device(tokens, value_weight, key_gate, query_gate, conv_filter, out_weight):
    hbm = pl.BlockSpec(memory_space=pl.ANY)
    vmem = pl.BlockSpec(memory_space=pltpu.VMEM)
    bf16, f32 = jnp.bfloat16, jnp.float32
    return pl.pallas_call(
        kernel,
        out_shape=jax.ShapeDtypeStruct((ROWS, WIDTH), bf16),
        in_specs=[hbm, hbm, hbm, hbm, vmem, hbm],
        out_specs=vmem,
        scratch_shapes=[
            pltpu.VMEM((17, WIDTH, WIDTH), bf16),
            pltpu.VMEM((17, WIDTH, WIDTH), bf16),
            pltpu.VMEM((8, ROWS, WIDTH), bf16),
            pltpu.VMEM((8, ROWS, WIDTH), bf16),
            pltpu.VMEM((WIDTH // GROUP * TAPS, 2 * TAPS), bf16),
            pltpu.VMEM((WIDTH // GROUP, 2 * TAPS), f32),
            pltpu.VMEM((TAPS + ROWS, WIDTH), bf16),
            pltpu.VMEM((ROWS, WIDTH), bf16),
            pltpu.VMEM((ROWS, WIDTH), bf16),
            pltpu.VMEM((ROWS, WIDTH), f32),
            pltpu.VMEM((ROWS, WIDTH), f32),
            pltpu.VMEM((2, ROWS, WIDTH), bf16),
            pltpu.VMEM((2, ROWS, WIDTH), bf16),
            pltpu.SemaphoreType.DMA((COPIES,)),
            pltpu.SemaphoreType.DMA((COPIES,)),
            pltpu.SemaphoreType.DMA((5,)),
        ],
        compiler_params=pltpu.CompilerParams(
            collective_id=0, has_side_effects=True, vmem_limit_bytes=56 * 1024 * 1024
        ),
        cost_estimate=pl.CostEstimate(flops=6_442_450_944, bytes_accessed=3_000_000, transcendentals=0),
        name="hyena_block",
    )(tokens, value_weight, key_gate, query_gate, conv_filter, out_weight)


def solution(mesh):
    return jax.shard_map(
        on_device,
        mesh=mesh,
        in_specs=(
            P("tok", "ch"),
            P("tok", "ch"),
            P("tok", "ch"),
            P("tok", "ch"),
            P("ch", None),
            P("tok", "ch"),
        ),
        out_specs=P("tok", "ch"),
        check_vma=False,
    )
```

time: 528 us -> 140 us (0.27)
  waiting for transfers between devices: 469 us -> 0 us
  Pallas kernels: 0 us -> 138 us
  matrix products: 22 us -> 0 us
  local copies, waits for them, and re-layouts: 19.8 us -> 1.77 us
  between operations: 13.3 us -> 0.01 us
    all_gather x4 -> x0, waiting for transfers between devices: 467 us -> none  [the longest x1 147 us: on_device(): gathered = lax.all_gather(tokens, 'ch', axis=1, tiled=True)]
    pallas_call x0 -> x1, Pallas kernels: none -> 138 us  [on_device(): pl.pallas_call(kernel, out_shape=jax.ShapeDtypeStruct((ROWS, WIDTH), bf16...]
    dot_general x4 -> x0, matrix products: 22 us -> none  [the longest x1 9.38 us: on_device(): jnp.dot(columns, lax.all_gather(out_weight, 'tok', axis=0, tiled=True), p...]
    reshape x1 -> x0, local copies, waits for them, and re-layouts: 9.72 us -> none  [banded_blocks(): tiled[:, :span * (period - 1)].reshape(groups_dev, span, period - 1)]
  transfers between devices with their start and end apart: 5 -> 0, of which waited for: 4 -> 0; matrix products, arithmetic and copies ran while one was open for 6% -> 0% of each run, Pallas kernels for 0% -> 0%
where the time goes in v1:
time: 140 us; the launch traced here: 139 us
  Pallas kernels  138 us (99%)
  local copies, waits for them, and re-layouts  1.77 us (1%)
    pallas_call x1, Pallas kernels, on_device(): pl.pallas_call(kernel, out_shape=jax.ShapeDtypeStruct((ROWS, WIDTH), bf16...  138 us

profile of v1, /device:TPU:1, one launch (start us, length us, event | category | flops | bytes accessed | tf_op | source)
XLA Modules:
  0.0 139.4 jit_solution(13908334003192836703)
XLA Ops:
  0.0 137.6 %hyena_block.1 = bf16[384,512]{1,0:T(8,128)(2,1)} custom-call(bf16[384,512]{1,0:T(8,128)(2,1)} %tok_hbm.1, bf16[512,512]{1,0:T(8,128)(2,1)} %wv_hbm.1, bf16[384,512]{1,0:T(8,128)(2,1)} %key_hbm.1, bf16[384,512]{1,0:T(8,128)(2,1)} %query_hbm.1, f32[32,128]{1,0:T(8,128)} %filt_ref.1, bf16[512,512]{1,0:T(8,128)(2,1)} %wo_hbm.1), custom_call_target="tpu_custom_call" | custom-call | flops 6442450944 | bytes 3000000 | tf_op jit(solution)/shard_map/hyena_block/pallas_call | solution.py:459
  137.6 1.8 %copy.8 = bf16[384,512]{1,0:T(8,128)(2,1)} copy(bf16[384,512]{1,0:T(8,128)(2,1)} %hyena_block.1) | data formatting | bytes 786432

commit v2 on v1

--- a/solution.py
+++ b/solution.py
@@ -12,9 +12,9 @@
 GROUP = 16
 ROWS = 384
 WIDTH = 512
-RELAY = 16
-WHOLE = ((0, 384),)
-PARTS = ((128, 256), (0, 128))
+HALF = WIDTH // 2
+CHUNKS = (((0, 192), (192, 192)), ((128, 256), (0, 128)))
+WHOLE = (0, ROWS)
 
 
 class Names:
@@ -55,13 +55,14 @@
     dev_z2 = place(x, y, zh * 4 + (1 - zl1) * 2 + zl0, c)
     far_zl0 = jnp.where(master, zl0, 1 - zl0)
     dev_far = place(x, y, (1 - zh) * 4 + zl1 * 2 + far_zl0, jnp.where(master, c, 1 - c))
+    dev_anti = place(x, y, (1 - zh) * 4 + zl, 1 - c)
     dev_sib = place(x, y, z, 1 - c)
     dev_next = (lax.rem(tok + 1, 16), ch)
     dev_prev = (lax.rem(tok + 15, 16), ch)
     dev_other = (jnp.where(c == 1, lax.rem(tok + 1, 16), lax.rem(tok + 15, 16)), ch)
 
     barrier = pltpu.get_barrier_semaphore()
-    partners = (dev_xp, dev_xm, dev_yp, dev_ym, dev_z1, dev_z2, dev_far, dev_sib, dev_other)
+    partners = (dev_xp, dev_xm, dev_yp, dev_ym, dev_z1, dev_z2, dev_far, dev_anti, dev_sib, dev_other)
     for d in partners:
         pl.semaphore_signal(barrier, inc=1, device_id=d, device_id_type=MESH)
     pl.semaphore_wait(barrier, len(partners))
@@ -78,35 +79,64 @@
     root_z = jnp.where(master, zh, 1 - zh)
     root_b = (jnp.where(master, own, away), jnp.where(master, away, own))
 
-    def copy(name, src, dst, dev):
-        i = names(name)
-        return pltpu.make_async_remote_copy(
-            src_ref=src, dst_ref=dst, send_sem=send_sem.at[i], recv_sem=recv_sem.at[i],
-            device_id=dev, device_id_type=MESH,
-        )
-
-    def w_in(m, recv=False):
-        dst = jnp.where(master, slot(away, zh, x), RELAY) if recv else jnp.where(master, RELAY, slot(own, zh, x))
-        return copy(("in", m), w_hbm[m], wbuf[m].at[dst], dev_z1)
-
-    def w_far(m, i, recv=False):
-        src = w_hbm[m] if i == 0 else wbuf[m].at[RELAY]
-        if recv:
-            dst = slot(away if i == 0 else own, 1 - zh, x)
-        else:
-            dst = slot(own if i == 0 else away, zh, x)
-        return copy(("far", m, i), src, wbuf[m].at[dst], dev_far)
-
-    def w_x(m, r, way, recv=False, native=False):
+    sent = {}
+    role = ["all"]
+
+    class Sent:
+        def __init__(self, name, src, dst, dev):
+            i = names(name)
+            self.name = name
+            self.make = lambda: pltpu.make_async_remote_copy(
+                src_ref=src, dst_ref=dst, send_sem=send_sem.at[i], recv_sem=recv_sem.at[i],
+                device_id=dev, device_id_type=MESH,
+            )
+
+        def start(self):
+            sent.setdefault(self.name, set()).add(role[0])
+            self.make().start()
+
+        def wait_recv(self):
+            self.make().wait_recv()
+
+        def wait_send(self):
+            self.make().wait_send()
+
+    copy = Sent
+
+    def when_master(body):
+        role[0] = "master"
+        pl.when(master)(body)
+        role[0] = "all"
+
+    def when_not(body):
+        role[0] = "nm"
+        pl.when(nm)(body)
+        role[0] = "all"
+
+    def half(h):
+        return pl.ds(h * HALF, HALF)
+
+    def w_in(m, h, recv=False):
+        s = slot(away if recv else own, zh, x)
+        return copy(("in", m, h), w_hbm[m].at[half(h)], wbuf[m].at[s, half(h)], dev_z1)
+
+    def w_far(m, h, recv=False):
+        s = slot(away, 1 - zh, x) if recv else slot(own, zh, x)
+        return copy(("far", m, h), w_hbm[m].at[half(h)], wbuf[m].at[s, half(h)], dev_far)
+
+    def w_anti(m, h, recv=False):
+        s = slot(own, 1 - zh, x) if recv else slot(own, zh, x)
+        return copy(("anti", m, h), w_hbm[m].at[half(h)], wbuf[m].at[s, half(h)], dev_anti)
+
+    def w_x(m, r, way, h, recv=False, native=False):
         from_x = (xm if way > 0 else xp) if recv else x
-        s = slot(root_b[r], root_z, from_x)
-        src = w_hbm[m] if native else wbuf[m].at[s]
-        return copy(("x", m, r, way), src, wbuf[m].at[s], dev_xp if way > 0 else dev_xm)
+        dst = wbuf[m].at[slot(root_b[r], root_z, from_x), half(h)]
+        src = w_hbm[m].at[half(h)] if native else dst
+        return copy(("x", m, r, way, h), src, dst, dev_xp if way > 0 else dev_xm)
 
     def w_fwd(m, r, way, recv=False):
         from_x = x2 if recv else (xm if way > 0 else xp)
-        rows = pl.ds(0, 256) if way > 0 else pl.ds(256, 256)
-        s = wbuf[m].at[slot(root_b[r], root_z, from_x), rows]
+        s = wbuf[m].at[slot(root_b[r], root_z, from_x), half(first_half(way))]
         return copy(("fwd", m, r, way), s, s, dev_xp if way > 0 else dev_xm)
 
     def w_sib(m, r, k, recv=False, native=False):
@@ -115,43 +145,56 @@
         src = w_hbm[m] if native else wbuf[m].at[s]
         return copy(("sib", m, r, k), src, wbuf[m].at[s], dev_sib)
 
-    def t_y(q, ch_, p, way, recv=False):
-        first, n = (WHOLE, PARTS)[q][ch_]
+    def first_half(way):
+        return 0 if way > 0 else 1
+
+    def t_y(q, ch_, p, way, h, recv=False):
+        first, n = CHUNKS[q][ch_]
         from_y = (ym if way > 0 else yp) if recv else y
         k = (zl1 if p == 0 else 1 - zl1) * 4 + from_y
-        ref = tbuf[q].at[k, pl.ds(first, n)]
-        src = tok_hbm if q == 0 and p == 0 else ref
-        return copy(("ty", q, ch_, p, way), src, ref, dev_yp if way > 0 else dev_ym)
+        rows = pl.ds(first + h * (n // 2), n // 2)
+        ref = tbuf[q].at[k, rows]
+        src = tok_hbm.at[rows] if q == 0 and p == 0 else ref
+        return copy(("ty", q, ch_, p, way, h), src, ref, dev_yp if way > 0 else dev_ym)
 
     def t_fwd(q, ch_, p, way, recv=False):
-        first, n = (WHOLE, PARTS)[q][ch_]
+        first, n = CHUNKS[q][ch_]
         from_y = y2 if recv else (ym if way > 0 else yp)
         k = (zl1 if p == 0 else 1 - zl1) * 4 + from_y
-        rows = pl.ds(first, n // 2) if way > 0 else pl.ds(first + n // 2, n // 2)
-        ref = tbuf[q].at[k, rows]
+        ref = tbuf[q].at[k, pl.ds(first + first_half(way) * (n // 2), n // 2)]
         return copy(("tfwd", q, ch_, p, way), ref, ref, dev_yp if way > 0 else dev_ym)
 
     def t_far(q, ch_, recv=False):
-        first, n = (WHOLE, PARTS)[q][ch_]
+        first, n = CHUNKS[q][ch_]
         ref = tbuf[q].at[((1 - zl1) if recv else zl1) * 4 + y, pl.ds(first, n)]
-        return copy(("tz", q, ch_), tok_hbm if q == 0 else ref, ref, dev_z2)
+        src = tok_hbm.at[pl.ds(first, n)] if q == 0 else ref
+        return copy(("tz", q, ch_), src, ref, dev_z2)
 
     def partial(q, ch_):
-        first, n = (WHOLE, PARTS)[q][ch_]
-        rows = pl.ds(first, n)
+        rows = pl.ds(*(WHOLE if q == 0 else CHUNKS[1][ch_]))
         return copy(("c", q, ch_), part_out.at[q, rows], part_in.at[q, rows], dev_z1)
 
     def halo():
         return copy(("halo",), ext.at[pl.ds(ROWS, TAPS)], ext.at[pl.ds(0, TAPS)], dev_next)
 
-    def both(make, *a):
-        for way in (1, -1):
-            make(*a, way).start()
+    senders = {
+        "in": w_in, "far": w_far, "anti": w_anti, "x": w_x, "fwd": w_fwd, "sib": w_sib,
+        "ty": t_y, "tfwd": t_fwd, "tz": t_far, "c": partial, "halo": halo,
+    }
+
+    def send_x(m, r, native=False):
+        for h in range(2):
+            for way in (1, -1):
+                w_x(m, r, way, h if way > 0 else 1 - h, native=native).start()
 
     def relay_x(m, r):
         for way in (1, -1):
-            w_x(m, r, way, recv=True).wait_recv()
+            w_x(m, r, way, first_half(way), recv=True).wait_recv()
             w_fwd(m, r, way).start()
+
+    def mid_x(m, r):
+        for way in (1, -1):
+            w_x(m, r, way, 1 - first_half(way), recv=True).wait_recv()
         w_sib(m, r, 1).start()
         w_sib(m, r, 2).start()
 
@@ -160,49 +203,44 @@
             w_fwd(m, r, way, recv=True).wait_recv()
         w_sib(m, r, 3).start()
 
-    def spread(m, r):
-        both(w_x, m, r)
+    def take_root(m, r, arrival):
+        for h in range(2):
+            arrival(m, h, recv=True).wait_recv()
+            for way in (1, -1):
+                w_x(m, r, way, h).start()
         w_sib(m, r, 0).start()
+
+    def send_y(q, ch_, p):
+        for h in range(2):
+            for way in (1, -1):
+                t_y(q, ch_, p, way, h if way > 0 else 1 - h).start()
 
     def relay_y(q, ch_, p):
         for way in (1, -1):
-            t_y(q, ch_, p, way, recv=True).wait_recv()
+            t_y(q, ch_, p, way, first_half(way), recv=True).wait_recv()
             t_fwd(q, ch_, p, way).start()
 
     def end_y(q, ch_, p):
         for way in (1, -1):
+            t_y(q, ch_, p, way, 1 - first_half(way), recv=True).wait_recv()
             t_fwd(q, ch_, p, way, recv=True).wait_recv()
 
-    def first_w(m):
-        w_in(m).start()
-
-        @pl.when(nm)
-        def _():
-            w_far(m, 0).start()
-
-    def native_w(m):
-        @pl.when(master)
-        def _():
-            for way in (1, -1):
-                w_x(m, 0, way, native=True).start()
-            w_sib(m, 0, 0, native=True).start()
-
-    def inbox_w(m):
-        w_in(m, recv=True).wait_recv()
-
-        @pl.when(master)
-        def _():
-            spread(m, 1)
-
-        @pl.when(nm)
-        def _():
-            w_far(m, 1).start()
-
-    def root_from_far(m, r):
-        @pl.when(nm)
-        def _():
-            w_far(m, r, recv=True).wait_recv()
-            spread(m, r)
+    def far_y(q, ch_):
+        t_far(q, ch_, recv=True).wait_recv()
+        send_y(q, ch_, 1)
+
+    def z_not(m):
+        for send in (w_in, w_far):
+            for h in range(2):
+                send(m, h).start()
+
+    def z_master(m):
+        for h in range(2):
+            w_anti(m, h).start()
+
+    def x_master(m):
+        send_x(m, 0, native=True)
+        w_sib(m, 0, 0, native=True).start()
 
     def local(i, src, dst):
         return pltpu.make_async_copy(src, dst, local_sem.at[i])
@@ -210,11 +248,24 @@
     def own_w(m):
         return local(m, w_hbm[m], wbuf[m].at[slot(own, zh, x)])
 
-    t_far(0, 0).start()
-    first_w(0)
-    for way in (1, -1):
-        t_y(0, 0, 0, way).start()
-    native_w(0)
+    for ch_ in range(2):
+        t_far(0, ch_).start()
+
+    @when_not
+    def _():
+        z_not(0)
+
+    @when_master
+    def _():
+        x_master(0)
+
+    for ch_ in range(2):
+        send_y(0, ch_, 0)
+
+    @when_master
+    def _():
+        z_master(0)
+
     own_tok = local(2, tok_hbm, tbuf[0].at[zl1 * 4 + y])
     own_key = local(3, key_hbm, key)
     own_query = local(4, query_hbm, query)
@@ -222,7 +273,7 @@
     own_key.start()
     own_query.start()
 
-    @pl.when(master)
+    @when_master
     def _():
         own_w(0).start()
         own_w(1).start()
@@ -254,53 +305,68 @@
         for k in range(4):
             w_sib(m, r, k, recv=True).wait_recv()
 
-    inbox_w(0)
     relay_y(0, 0, 0)
-
-    @pl.when(master)
+    relay_y(0, 1, 0)
+
+    @when_master
     def _():
         relay_x(0, 0)
-
-    root_from_far(0, 0)
-    t_far(0, 0, recv=True).wait_recv()
-    both(t_y, 0, 0, 1)
-
-    @pl.when(master)
+        take_root(0, 1, w_in)
+        mid_x(0, 0)
+
+    far_y(0, 0)
+
+    @when_not
+    def _():
+        take_root(0, 0, w_far)
+
+    far_y(0, 1)
+
+    @when_master
     def _():
         end_x(0, 0)
         relay_x(0, 1)
-
-    @pl.when(nm)
+        x_master(1)
+
+    @when_not
     def _():
         relay_x(0, 0)
 
-    root_from_far(0, 1)
-    first_w(1)
-    native_w(1)
     relay_y(0, 0, 1)
-    end_y(0, 0, 0)
-
-    @pl.when(master)
-    def _():
+
+    @when_not
+    def _():
+        take_root(0, 1, w_anti)
+        z_not(1)
+
+    relay_y(0, 1, 1)
+
+    @when_master
+    def _():
+        mid_x(0, 1)
         end_x(0, 1)
-
-    @pl.when(nm)
-    def _():
+        z_master(1)
+
+    @when_not
+    def _():
+        mid_x(0, 0)
         end_x(0, 0)
         relay_x(0, 1)
 
     own_tok.wait()
-    end_y(0, 0, 1)
+    for p in range(2):
+        for ch_ in range(2):
+            end_y(0, ch_, p)
 
     every = pl.ds(0, ROWS)
 
-    @pl.when(master)
+    @when_master
     def _():
         own_w(0).wait()
         own_w(1).wait()
         wait_sib(0, 0)
 
-    @pl.when(nm)
+    @when_not
     def _():
         wait_sib(0, 1)
 
@@ -308,22 +374,25 @@
         multiply(0, acc_away, every, away, zz)
     part_out[0] = acc_away[...].astype(jnp.bfloat16)
     partial(0, 0).start()
-    inbox_w(1)
-
-    @pl.when(master)
+
+    @when_master
     def _():
         relay_x(1, 0)
+        take_root(1, 1, w_in)
         wait_sib(0, 1)
 
-    @pl.when(nm)
-    def _():
+    @when_not
+    def _():
+        mid_x(0, 1)
         end_x(0, 1)
         wait_sib(0, 0)
 
     for zz in range(2):
         multiply(0, acc_own, every, own, zz)
 
-    root_from_far(1, 0)
+    @when_not
+    def _():
+        take_root(1, 0, w_far)
 
     own_key.wait()
     own_query.wait()
@@ -355,12 +424,11 @@
 
     def send_shaped(ch_):
         t_far(1, ch_).start()
-        both(t_y, 1, ch_, 0)
+        send_y(1, ch_, 0)
 
     convolve(1)
     convolve(2)
     send_shaped(0)
-    root_from_far(1, 1)
     halo().wait_recv()
 
     @pl.when(tok == 0)
@@ -370,46 +438,52 @@
     convolve(0)
     send_shaped(1)
 
-    @pl.when(master)
-    def _():
+    @when_master
+    def _():
+        mid_x(1, 0)
         end_x(1, 0)
         relay_x(1, 1)
 
+    @when_not
+    def _():
+        relay_x(1, 0)
+
     relay_y(1, 0, 0)
-    t_far(1, 0, recv=True).wait_recv()
-    both(t_y, 1, 0, 1)
-
-    @pl.when(nm)
-    def _():
-        relay_x(1, 0)
+    far_y(1, 0)
+
+    @when_not
+    def _():
+        take_root(1, 1, w_anti)
 
     relay_y(1, 1, 0)
-    t_far(1, 1, recv=True).wait_recv()
-    both(t_y, 1, 1, 1)
-
-    @pl.when(master)
-    def _():
+    far_y(1, 1)
+
+    @when_master
+    def _():
+        mid_x(1, 1)
         end_x(1, 1)
 
-    @pl.when(nm)
-    def _():
+    @when_not
+    def _():
+        mid_x(1, 0)
+        end_x(1, 0)
         relay_x(1, 1)
-        end_x(1, 0)
 
     relay_y(1, 0, 1)
     end_y(1, 0, 0)
-
-    @pl.when(nm)
-    def _():
+    relay_y(1, 1, 1)
+
+    @when_not
+    def _():
+        mid_x(1, 1)
         end_x(1, 1)
 
-    relay_y(1, 1, 1)
     end_y(1, 0, 1)
     wait_sib(1, 0)
     wait_sib(1, 1)
 
     for ch_ in range(2):
-        rows = pl.ds(*PARTS[ch_])
+        rows = pl.ds(*CHUNKS[1][ch_])
         if ch_ == 1:
             end_y(1, 1, 0)
             end_y(1, 1, 1)
@@ -420,36 +494,27 @@
         for zz in range(2):
             multiply(1, acc_own, rows, own, zz)
     for ch_ in range(2):
-        rows = pl.ds(*PARTS[ch_])
+        rows = pl.ds(*CHUNKS[1][ch_])
         partial(1, ch_).wait_recv()
         out_ref[rows] = (acc_own[rows] + part_in[1, rows].astype(jnp.float32)).astype(jnp.bfloat16)
 
-    for m in range(2):
-        w_in(m).wait_send()
-        for r in range(2):
-            for way in (1, -1):
-                w_x(m, r, way).wait_send()
-                w_fwd(m, r, way).wait_send()
-            for k in range(4):
-                w_sib(m, r, k).wait_send()
-
-        @pl.when(nm)
-        def _():
-            w_far(m, 0).wait_send()
-            w_far(m, 1).wait_send()
-
-    for q, parts in ((0, WHOLE), (1, PARTS)):
-        for ch_ in range(len(parts)):
-            for p in range(2):
-                for way in (1, -1):
-                    t_y(q, ch_, p, way).wait_send()
-                    t_fwd(q, ch_, p, way).wait_send()
-            t_far(q, ch_).wait_send()
-            partial(q, ch_).wait_send()
-    halo().wait_send()
-
-
-COPIES = 96
+    def last(only):
+        for name, roles in sent.items():
+            if ("all" in roles or len(roles) == 2) == (only == "all") and (only == "all" or only in roles):
+                senders[name[0]](*name[1:]).wait_send()
+
+    last("all")
+
+    @when_master
+    def _():
+        last("master")
+
+    @when_not
+    def _():
+        last("nm")
+
+
+COPIES = 128
 
 
 def on_device(tokens, value_weight, key_gate, query_gate, conv_filter, out_weight):
@@ -462,8 +527,8 @@
         in_specs=[hbm, hbm, hbm, hbm, vmem, hbm],
         out_specs=vmem,
         scratch_shapes=[
-            pltpu.VMEM((17, WIDTH, WIDTH), bf16),
-            pltpu.VMEM((17, WIDTH, WIDTH), bf16),
+            pltpu.VMEM((16, WIDTH, WIDTH), bf16),
+            pltpu.VMEM((16, WIDTH, WIDTH), bf16),
             pltpu.VMEM((8, ROWS, WIDTH), bf16),
             pltpu.VMEM((8, ROWS, WIDTH), bf16),
             pltpu.VMEM((WIDTH // GROUP * TAPS, 2 * TAPS), bf16),

time: 140 us -> 137 us (0.979)
  Pallas kernels: 138 us -> 135 us
    pallas_call x1, Pallas kernels: 138 us -> 135 us  [on_device(): pl.pallas_call(kernel, out_shape=jax.ShapeDtypeStruct((ROWS, WIDTH), bf16...]
where the time goes in v2:
time: 137 us
  Pallas kernels  135 us (99%)
  local copies, waits for them, and re-layouts  1.77 us (1%)
    pallas_call x1, Pallas kernels, on_device(): pl.pallas_call(kernel, out_shape=jax.ShapeDtypeStruct((ROWS, WIDTH), bf16...  135 us

profile of v2, /device:TPU:1, one launch (start us, length us, event | category | flops | bytes accessed | tf_op | source)
XLA Modules:
  0.0 136.8 jit_solution(2049769932538010316)
XLA Ops:
  0.0 135.0 %hyena_block.1 = bf16[384,512]{1,0:T(8,128)(2,1)} custom-call(bf16[384,512]{1,0:T(8,128)(2,1)} %tok_hbm.1, bf16[512,512]{1,0:T(8,128)(2,1)} %wv_hbm.1, bf16[384,512]{1,0:T(8,128)(2,1)} %key_hbm.1, bf16[384,512]{1,0:T(8,128)(2,1)} %query_hbm.1, f32[32,128]{1,0:T(8,128)} %filt_ref.1, bf16[512,512]{1,0:T(8,128)(2,1)} %wo_hbm.1), custom_call_target="tpu_custom_call" | custom-call | flops 6442450944 | bytes 3000000 | tf_op jit(solution)/shard_map/hyena_block/pallas_call | solution.py:524
  135.0 1.8 %copy.8 = bf16[384,512]{1,0:T(8,128)(2,1)} copy(bf16[384,512]{1,0:T(8,128)(2,1)} %hyena_block.1) | data formatting | bytes 786432

commit v3 on v2

--- a/solution.py
+++ b/solution.py
@@ -203,12 +203,12 @@
             w_fwd(m, r, way, recv=True).wait_recv()
         w_sib(m, r, 3).start()
 
-    def take_root(m, r, arrival):
-        for h in range(2):
-            arrival(m, h, recv=True).wait_recv()
-            for way in (1, -1):
-                w_x(m, r, way, h).start()
-        w_sib(m, r, 0).start()
+    def take_half(m, r, h, arrival):
+        arrival(m, h, recv=True).wait_recv()
+        for way in (1, -1):
+            w_x(m, r, way, h).start()
+        if h == 1:
+            w_sib(m, r, 0).start()
 
     def send_y(q, ch_, p):
         for h in range(2):
@@ -229,14 +229,17 @@
         t_far(q, ch_, recv=True).wait_recv()
         send_y(q, ch_, 1)
 
-    def z_not(m):
-        for send in (w_in, w_far):
-            for h in range(2):
-                send(m, h).start()
-
-    def z_master(m):
-        for h in range(2):
-            w_anti(m, h).start()
+    def z_in(m, h):
+        w_in(m, h).start()
+
+    def z_far(m, h):
+        w_far(m, h).start()
+
+    def z_anti(m, h):
+        w_anti(m, h).start()
+
+    def t_z(ch_):
+        t_far(0, ch_).start()
 
     def x_master(m):
         send_x(m, 0, native=True)
@@ -248,23 +251,22 @@
     def own_w(m):
         return local(m, w_hbm[m], wbuf[m].at[slot(own, zh, x)])
 
-    for ch_ in range(2):
-        t_far(0, ch_).start()
-
-    @when_not
-    def _():
-        z_not(0)
+
+    @when_not
+    def _():
+        z_in(0, 0)
+
 
     @when_master
     def _():
         x_master(0)
 
-    for ch_ in range(2):
-        send_y(0, ch_, 0)
-
-    @when_master
-    def _():
-        z_master(0)
+    t_z(0)
+
+    @when_not
+    def _():
+        z_far(0, 0)
+
 
     own_tok = local(2, tok_hbm, tbuf[0].at[zl1 * 4 + y])
     own_key = local(3, key_hbm, key)
@@ -293,210 +295,309 @@
     acc_own[...] = jnp.zeros_like(acc_own)
 
     def multiply(q, acc, rows, b, zz):
-        @pl.loop(0, 4)
-        def _(j):
-            lhs = tbuf[q][zz * 4 + j, rows, :]
-            w = wbuf[q].at[slot(b, zz, j)]
-            for n in range(2):
-                cols = pl.ds(n * 256, 256)
-                acc[rows, cols] += jnp.dot(lhs, w[:, cols], preferred_element_type=jnp.float32)
+        for n in range(2):
+            cols = pl.ds(n * 256, 256)
+            total = None
+            for j in range(4):
+                term = jnp.dot(
+                    tbuf[q][zz * 4 + j, rows, :],
+                    wbuf[q][slot(b, zz, j), :, cols],
+                    preferred_element_type=jnp.float32,
+                )
+                total = term if total is None else total + term
+            acc[rows, cols] += total
 
     def wait_sib(m, r):
         for k in range(4):
             w_sib(m, r, k, recv=True).wait_recv()
 
-    relay_y(0, 0, 0)
-    relay_y(0, 1, 0)
-
-    @when_master
-    def _():
-        relay_x(0, 0)
-        take_root(0, 1, w_in)
-        mid_x(0, 0)
-
-    far_y(0, 0)
-
-    @when_not
-    def _():
-        take_root(0, 0, w_far)
-
-    far_y(0, 1)
-
-    @when_master
-    def _():
-        end_x(0, 0)
-        relay_x(0, 1)
-        x_master(1)
-
-    @when_not
-    def _():
-        relay_x(0, 0)
-
-    relay_y(0, 0, 1)
-
-    @when_not
-    def _():
-        take_root(0, 1, w_anti)
-        z_not(1)
-
-    relay_y(0, 1, 1)
-
-    @when_master
-    def _():
-        mid_x(0, 1)
-        end_x(0, 1)
-        z_master(1)
-
-    @when_not
-    def _():
-        mid_x(0, 0)
-        end_x(0, 0)
-        relay_x(0, 1)
-
-    own_tok.wait()
-    for p in range(2):
-        for ch_ in range(2):
-            end_y(0, ch_, p)
-
     every = pl.ds(0, ROWS)
-
-    @when_master
-    def _():
-        own_w(0).wait()
-        own_w(1).wait()
-        wait_sib(0, 0)
-
-    @when_not
-    def _():
-        wait_sib(0, 1)
-
-    for zz in range(2):
-        multiply(0, acc_away, every, away, zz)
-    part_out[0] = acc_away[...].astype(jnp.bfloat16)
-    partial(0, 0).start()
-
-    @when_master
-    def _():
-        relay_x(1, 0)
-        take_root(1, 1, w_in)
-        wait_sib(0, 1)
-
-    @when_not
-    def _():
-        mid_x(0, 1)
-        end_x(0, 1)
-        wait_sib(0, 0)
-
-    for zz in range(2):
-        multiply(0, acc_own, every, own, zz)
-
-    @when_not
-    def _():
-        take_root(1, 0, w_far)
-
-    own_key.wait()
-    own_query.wait()
-    partial(0, 0).wait_recv()
-    values = (acc_own[...] + part_in[0].astype(jnp.float32)).astype(jnp.bfloat16)
-    ext[pl.ds(TAPS, ROWS), :] = (values.astype(jnp.float32) * key[...].astype(jnp.float32)).astype(jnp.bfloat16)
-    halo().start()
-    acc_away[...] = jnp.zeros_like(acc_away)
-    acc_own[...] = jnp.zeros_like(acc_own)
-
-    lane_group = lax.broadcasted_iota(jnp.int32, (TAPS, TAPS), 1) // GROUP
     k_own = zl1 * 4 + y
 
-    def convolve(block):
-        first = block * TAPS
+    def convolve(blocks):
+        width = len(blocks) * TAPS
+        lane_group = lax.rem(lax.broadcasted_iota(jnp.int32, (TAPS, width), 1), TAPS) // GROUP
         for tile in range(WIDTH // TAPS):
             lanes = pl.ds(tile * TAPS, TAPS)
-            raw = jnp.dot(
-                band[pl.ds(tile * 8 * TAPS, 8 * TAPS), :],
-                ext[pl.ds(first, 2 * TAPS), lanes],
-                preferred_element_type=jnp.float32,
-            )
-            conv = raw[:TAPS]
-            for g in range(1, 8):
-                conv = jnp.where(lane_group == g, raw[g * TAPS : (g + 1) * TAPS], conv)
-            rows = pl.ds(first, TAPS)
-            shaped = conv * query[rows, lanes].astype(jnp.float32)
-            tbuf_o[k_own, rows, lanes] = shaped.astype(jnp.bfloat16)
+            parts = [ext[pl.ds(block * TAPS, 2 * TAPS), lanes] for block in blocks]
+            window = parts[0] if len(parts) == 1 else jnp.concatenate(parts, axis=1)
+            conv = None
+            for g in range(8):
+                raw = jnp.dot(
+                    band[pl.ds((tile * 8 + g) * TAPS, TAPS), :], window, preferred_element_type=jnp.float32
+                )
+                conv = raw if conv is None else jnp.where(lane_group == g, raw, conv)
+            for i, block in enumerate(blocks):
+                rows = pl.ds(block * TAPS, TAPS)
+                shaped = conv[:, i * TAPS : (i + 1) * TAPS] * query[rows, lanes].astype(jnp.float32)
+                tbuf_o[k_own, rows, lanes] = shaped.astype(jnp.bfloat16)
 
     def send_shaped(ch_):
         t_far(1, ch_).start()
         send_y(1, ch_, 0)
 
-    convolve(1)
-    convolve(2)
-    send_shaped(0)
-    halo().wait_recv()
-
-    @pl.when(tok == 0)
-    def _():
-        ext[pl.ds(0, TAPS), :] = jnp.zeros((TAPS, WIDTH), jnp.bfloat16)
-
-    convolve(0)
-    send_shaped(1)
-
-    @when_master
-    def _():
-        mid_x(1, 0)
-        end_x(1, 0)
-        relay_x(1, 1)
-
-    @when_not
-    def _():
-        relay_x(1, 0)
-
-    relay_y(1, 0, 0)
-    far_y(1, 0)
-
-    @when_not
-    def _():
-        take_root(1, 1, w_anti)
-
-    relay_y(1, 1, 0)
-    far_y(1, 1)
-
-    @when_master
-    def _():
-        mid_x(1, 1)
-        end_x(1, 1)
-
-    @when_not
-    def _():
-        mid_x(1, 0)
-        end_x(1, 0)
-        relay_x(1, 1)
-
-    relay_y(1, 0, 1)
-    end_y(1, 0, 0)
-    relay_y(1, 1, 1)
-
-    @when_not
-    def _():
-        mid_x(1, 1)
-        end_x(1, 1)
-
-    end_y(1, 0, 1)
-    wait_sib(1, 0)
-    wait_sib(1, 1)
-
-    for ch_ in range(2):
+    def away0():
+        own_tok.wait()
+
+        @pl.when(master)
+        def _():
+            own_w(0).wait()
+            own_w(1).wait()
+
+        for zz in range(2):
+            multiply(0, acc_away, every, away, zz)
+        part_out[0] = acc_away[...].astype(jnp.bfloat16)
+        partial(0, 0).start()
+        acc_away[...] = jnp.zeros_like(acc_away)
+
+    def own0():
+        for zz in range(2):
+            multiply(0, acc_own, every, own, zz)
+
+    def gate():
+        own_key.wait()
+        own_query.wait()
+        partial(0, 0).wait_recv()
+        values = (acc_own[...] + part_in[0].astype(jnp.float32)).astype(jnp.bfloat16)
+        ext[pl.ds(TAPS, ROWS), :] = (values.astype(jnp.float32) * key[...].astype(jnp.float32)).astype(jnp.bfloat16)
+        halo().start()
+        convolve((1, 2))
+        send_shaped(0)
+        acc_own[...] = jnp.zeros_like(acc_own)
+
+    def rim():
+        halo().wait_recv()
+
+        @pl.when(tok == 0)
+        def _():
+            ext[pl.ds(0, TAPS), :] = jnp.zeros((TAPS, WIDTH), jnp.bfloat16)
+
+        convolve((0,))
+        send_shaped(1)
+
+    def near2(ch_):
         rows = pl.ds(*CHUNKS[1][ch_])
-        if ch_ == 1:
-            end_y(1, 1, 0)
-            end_y(1, 1, 1)
-        for zz in range(2):
-            multiply(1, acc_away, rows, away, zz)
+        multiply(1, acc_away, rows, away, zl1)
+        multiply(1, acc_own, rows, own, zl1)
+
+    def far2(ch_):
+        rows = pl.ds(*CHUNKS[1][ch_])
+        multiply(1, acc_away, rows, away, 1 - zl1)
         part_out[1, rows] = acc_away[rows].astype(jnp.bfloat16)
         partial(1, ch_).start()
-        for zz in range(2):
-            multiply(1, acc_own, rows, own, zz)
-    for ch_ in range(2):
+        multiply(1, acc_own, rows, own, 1 - zl1)
+
+    def result(ch_):
         rows = pl.ds(*CHUNKS[1][ch_])
         partial(1, ch_).wait_recv()
         out_ref[rows] = (acc_own[rows] + part_in[1, rows].astype(jnp.float32)).astype(jnp.bfloat16)
+
+
+    @when_master
+    def _():
+        x_master(1)
+
+    send_y(0, 0, 0)
+
+    @when_master
+    def _():
+        take_half(0, 1, 0, w_in)
+        take_half(0, 1, 1, w_in)
+        z_anti(0, 1)
+
+
+    @when_not
+    def _():
+        z_in(0, 1)
+
+    relay_y(0, 0, 0)
+    send_y(0, 1, 0)
+
+    @when_master
+    def _():
+        relay_x(0, 0)
+        end_x(0, 0)
+        relay_x(0, 1)
+
+
+    @when_not
+    def _():
+        z_far(0, 1)
+
+    relay_y(0, 1, 0)
+
+    @when_master
+    def _():
+        z_anti(0, 0)
+
+
+    @when_not
+    def _():
+        z_in(1, 1)
+
+    far_y(0, 0)
+
+    @when_master
+    def _():
+        mid_x(0, 0)
+
+
+    @when_not
+    def _():
+        take_half(0, 0, 0, w_far)
+
+    t_z(1)
+
+    @when_not
+    def _():
+        take_half(0, 0, 1, w_far)
+
+    far_y(0, 1)
+    end_y(0, 0, 0)
+
+    @when_master
+    def _():
+        mid_x(0, 1)
+        z_anti(1, 0)
+        end_x(0, 1)
+
+    relay_y(0, 1, 1)
+    relay_y(0, 0, 1)
+
+    @when_master
+    def _():
+        take_half(1, 1, 0, w_in)
+        wait_sib(0, 0)
+
+
+    @when_not
+    def _():
+        relay_x(0, 0)
+        z_far(1, 0)
+        take_half(0, 1, 0, w_anti)
+        z_in(1, 0)
+        z_far(1, 1)
+        take_half(0, 1, 1, w_anti)
+
+    end_y(0, 1, 1)
+
+    @when_not
+    def _():
+        mid_x(0, 0)
+        end_x(0, 0)
+
+    end_y(0, 0, 1)
+
+    @when_not
+    def _():
+        relay_x(0, 1)
+
+    end_y(0, 1, 0)
+
+    @when_not
+    def _():
+        mid_x(0, 1)
+        wait_sib(0, 1)
+        wait_sib(0, 0)
+
+    away0()
+
+    @when_master
+    def _():
+        wait_sib(0, 1)
+        take_half(1, 1, 1, w_in)
+
+
+    @when_not
+    def _():
+        take_half(1, 0, 0, w_far)
+        end_x(0, 1)
+        take_half(1, 1, 0, w_anti)
+
+    own0()
+
+    @when_master
+    def _():
+        z_anti(1, 1)
+        relay_x(1, 1)
+        relay_x(1, 0)
+
+
+    @when_not
+    def _():
+        take_half(1, 0, 1, w_far)
+
+    gate()
+
+    @when_master
+    def _():
+        mid_x(1, 0)
+
+    relay_y(1, 0, 0)
+
+    @when_master
+    def _():
+        end_x(1, 0)
+
+
+    @when_not
+    def _():
+        relay_x(1, 0)
+
+    rim()
+
+    @when_master
+    def _():
+        mid_x(1, 1)
+
+    far_y(1, 0)
+    relay_y(1, 1, 0)
+
+    @when_master
+    def _():
+        end_x(1, 1)
+
+
+    @when_not
+    def _():
+        take_half(1, 1, 1, w_anti)
+
+    far_y(1, 1)
+
+    @when_not
+    def _():
+        relay_x(1, 1)
+
+    relay_y(1, 0, 1)
+
+    @when_not
+    def _():
+        end_x(1, 0)
+
+    end_y(1, 0, 0)
+
+    @when_not
+    def _():
+        mid_x(1, 0)
+
+    wait_sib(1, 1)
+
+    @when_not
+    def _():
+        mid_x(1, 1)
+        end_x(1, 1)
+
+    wait_sib(1, 0)
+    end_y(1, 1, 0)
+    near2(1)
+    near2(0)
+    relay_y(1, 1, 1)
+    end_y(1, 0, 1)
+    far2(0)
+    end_y(1, 1, 1)
+    far2(1)
+    result(1)
+    result(0)
 
     def last(only):
         for name, roles in sent.items():

time: 137 us -> 134 us (0.978)
  the two profiles are of different devices: /device:TPU:1 before, /device:TPU:69 now
where the time goes in v3:
time: 134 us
  Pallas kernels  132 us (99%)
  local copies, waits for them, and re-layouts  1.77 us (1%)
    pallas_call x1, Pallas kernels, on_device(): pl.pallas_call(kernel, out_shape=jax.ShapeDtypeStruct((ROWS, WIDTH), bf16...  132 us

profile of v3, /device:TPU:69, one launch (start us, length us, event | category | flops | bytes accessed | tf_op | source)
XLA Modules:
  0.0 133.9 jit_solution(13016921754813960565)
XLA Ops:
  0.0 132.1 %hyena_block.1 = bf16[384,512]{1,0:T(8,128)(2,1)} custom-call(bf16[384,512]{1,0:T(8,128)(2,1)} %tok_hbm.1, bf16[512,512]{1,0:T(8,128)(2,1)} %wv_hbm.1, bf16[384,512]{1,0:T(8,128)(2,1)} %key_hbm.1, bf16[384,512]{1,0:T(8,128)(2,1)} %query_hbm.1, f32[32,128]{1,0:T(8,128)} %filt_ref.1, bf16[512,512]{1,0:T(8,128)(2,1)} %wo_hbm.1), custom_call_target="tpu_custom_call" | custom-call | flops 6442450944 | bytes 3000000 | tf_op jit(solution)/shard_map/hyena_block/pallas_call | solution.py:625
  132.1 1.8 %copy.8 = bf16[384,512]{1,0:T(8,128)(2,1)} copy(bf16[384,512]{1,0:T(8,128)(2,1)} %hyena_block.1) | data formatting | bytes 786432

commit v4 on v3

--- a/solution.py
+++ b/solution.py
@@ -13,7 +13,8 @@
 ROWS = 384
 WIDTH = 512
 HALF = WIDTH // 2
-CHUNKS = (((0, 192), (192, 192)), ((128, 256), (0, 128)))
+RELAY = 16
+CHUNKS = (((0, 192), (192, 192)), ((128, 128), (256, 128), (0, 128)))
 WHOLE = (0, ROWS)
 
 
@@ -55,14 +56,13 @@
     dev_z2 = place(x, y, zh * 4 + (1 - zl1) * 2 + zl0, c)
     far_zl0 = jnp.where(master, zl0, 1 - zl0)
     dev_far = place(x, y, (1 - zh) * 4 + zl1 * 2 + far_zl0, jnp.where(master, c, 1 - c))
-    dev_anti = place(x, y, (1 - zh) * 4 + zl, 1 - c)
     dev_sib = place(x, y, z, 1 - c)
     dev_next = (lax.rem(tok + 1, 16), ch)
     dev_prev = (lax.rem(tok + 15, 16), ch)
     dev_other = (jnp.where(c == 1, lax.rem(tok + 1, 16), lax.rem(tok + 15, 16)), ch)
 
     barrier = pltpu.get_barrier_semaphore()
-    partners = (dev_xp, dev_xm, dev_yp, dev_ym, dev_z1, dev_z2, dev_far, dev_anti, dev_sib, dev_other)
+    partners = (dev_xp, dev_xm, dev_yp, dev_ym, dev_z1, dev_z2, dev_far, dev_sib, dev_other)
     for d in partners:
         pl.semaphore_signal(barrier, inc=1, device_id=d, device_id_type=MESH)
     pl.semaphore_wait(barrier, len(partners))
@@ -124,9 +124,12 @@
         s = slot(away, 1 - zh, x) if recv else slot(own, zh, x)
         return copy(("far", m, h), w_hbm[m].at[half(h)], wbuf[m].at[s, half(h)], dev_far)
 
+    def w_pre(m, h):
+        return copy(("pre", m, h), w_hbm[m].at[half(h)], wbuf[m].at[RELAY, half(h)], dev_z1)
+
     def w_anti(m, h, recv=False):
-        s = slot(own, 1 - zh, x) if recv else slot(own, zh, x)
-        return copy(("anti", m, h), w_hbm[m].at[half(h)], wbuf[m].at[s, half(h)], dev_anti)
+        s = slot(own, 1 - zh, x) if recv else slot(away, zh, x)
+        return copy(("anti", m, h), wbuf[m].at[RELAY, half(h)], wbuf[m].at[s, half(h)], dev_far)
 
     def w_x(m, r, way, h, recv=False, native=False):
         from_x = (xm if way > 0 else xp) if recv else x
@@ -178,7 +181,7 @@
         return copy(("halo",), ext.at[pl.ds(ROWS, TAPS)], ext.at[pl.ds(0, TAPS)], dev_next)
 
     senders = {
-        "in": w_in, "far": w_far, "anti": w_anti, "x": w_x, "fwd": w_fwd, "sib": w_sib,
+        "in": w_in, "far": w_far, "pre": w_pre, "anti": w_anti, "x": w_x, "fwd": w_fwd, "sib": w_sib,
         "ty": t_y, "tfwd": t_fwd, "tz": t_far, "c": partial, "halo": halo,
     }
 
@@ -235,7 +238,11 @@
     def z_far(m, h):
         w_far(m, h).start()
 
-    def z_anti(m, h):
+    def z_pre(m, h):
+        w_pre(m, h).start()
+
+    def pass_on(m, h):
+        w_pre(m, h).wait_recv()
         w_anti(m, h).start()
 
     def t_z(ch_):
@@ -254,18 +261,13 @@
 
     @when_not
     def _():
+        z_far(0, 0)
         z_in(0, 0)
 
 
     @when_master
     def _():
         x_master(0)
-
-    t_z(0)
-
-    @when_not
-    def _():
-        z_far(0, 0)
 
 
     own_tok = local(2, tok_hbm, tbuf[0].at[zl1 * 4 + y])
@@ -350,9 +352,8 @@
         partial(0, 0).start()
         acc_away[...] = jnp.zeros_like(acc_away)
 
-    def own0():
-        for zz in range(2):
-            multiply(0, acc_own, every, own, zz)
+    def own0(zz):
+        multiply(0, acc_own, every, own, zz)
 
     def gate():
         own_key.wait()
@@ -363,6 +364,7 @@
         halo().start()
         convolve((1, 2))
         send_shaped(0)
+        send_shaped(1)
         acc_own[...] = jnp.zeros_like(acc_own)
 
     def rim():
@@ -373,7 +375,7 @@
             ext[pl.ds(0, TAPS), :] = jnp.zeros((TAPS, WIDTH), jnp.bfloat16)
 
         convolve((0,))
-        send_shaped(1)
+        send_shaped(2)
 
     def near2(ch_):
         rows = pl.ds(*CHUNKS[1][ch_])
@@ -395,209 +397,202 @@
 
     @when_master
     def _():
+        relay_x(0, 0)
+        take_half(0, 1, 0, w_in)
         x_master(1)
-
-    send_y(0, 0, 0)
-
-    @when_master
-    def _():
-        take_half(0, 1, 0, w_in)
+        z_pre(0, 0)
+        send_y(0, 0, 0)
+        relay_y(0, 0, 0)
         take_half(0, 1, 1, w_in)
-        z_anti(0, 1)
-
-
-    @when_not
-    def _():
+        t_z(0)
+        relay_x(0, 1)
+        z_pre(0, 1)
+        t_z(1)
+        relay_x(1, 0)
+        end_y(0, 0, 0)
+        z_pre(1, 0)
+        far_y(0, 0)
+        end_x(0, 0)
+        far_y(0, 1)
+        mid_x(0, 1)
+        end_x(0, 1)
+        z_pre(1, 1)
+        relay_y(0, 1, 1)
+        mid_x(0, 0)
+        send_y(0, 1, 0)
+        relay_y(0, 0, 1)
+        end_y(0, 1, 1)
+        take_half(1, 1, 0, w_in)
+        mid_x(1, 0)
+        relay_y(0, 1, 0)
+        end_y(0, 0, 1)
+        end_y(0, 1, 0)
+        take_half(1, 1, 1, w_in)
+        end_x(1, 0)
+        wait_sib(0, 0)
+
+
+    @when_not
+    def _():
+        z_far(0, 1)
+        t_z(0)
+        send_y(0, 0, 0)
+        relay_y(0, 0, 0)
         z_in(0, 1)
-
-    relay_y(0, 0, 0)
-    send_y(0, 1, 0)
-
-    @when_master
-    def _():
+        t_z(1)
+        end_y(0, 0, 0)
+        z_in(1, 1)
+        far_y(0, 1)
+        take_half(0, 0, 0, w_far)
+        send_y(0, 1, 0)
+        far_y(0, 0)
+        pass_on(0, 0)
+        pass_on(0, 1)
+        take_half(0, 0, 1, w_far)
+        relay_y(0, 1, 1)
+        z_far(1, 0)
+        relay_y(0, 0, 1)
         relay_x(0, 0)
+        mid_x(0, 0)
+        end_y(0, 1, 1)
+        relay_y(0, 1, 0)
+        take_half(0, 1, 0, w_anti)
         end_x(0, 0)
+        end_y(0, 0, 1)
+        z_in(1, 0)
+        wait_sib(0, 1)
+        end_y(0, 1, 0)
+        take_half(0, 1, 1, w_anti)
+        z_far(1, 1)
+
+    away0()
+
+    @when_master
+    def _():
+        wait_sib(0, 1)
+
+
+    @when_not
+    def _():
+        wait_sib(0, 0)
+
+    own0(zh)
+
+    @when_master
+    def _():
+        relay_x(1, 1)
+
+
+    @when_not
+    def _():
         relay_x(0, 1)
-
-
-    @when_not
-    def _():
-        z_far(0, 1)
-
-    relay_y(0, 1, 0)
-
-    @when_master
-    def _():
-        z_anti(0, 0)
-
-
-    @when_not
-    def _():
-        z_in(1, 1)
-
-    far_y(0, 0)
-
-    @when_master
-    def _():
-        mid_x(0, 0)
-
-
-    @when_not
-    def _():
-        take_half(0, 0, 0, w_far)
-
-    t_z(1)
-
-    @when_not
-    def _():
-        take_half(0, 0, 1, w_far)
-
-    far_y(0, 1)
-    end_y(0, 0, 0)
-
-    @when_master
-    def _():
         mid_x(0, 1)
-        z_anti(1, 0)
-        end_x(0, 1)
-
-    relay_y(0, 1, 1)
-    relay_y(0, 0, 1)
-
-    @when_master
-    def _():
-        take_half(1, 1, 0, w_in)
-        wait_sib(0, 0)
-
-
-    @when_not
-    def _():
-        relay_x(0, 0)
-        z_far(1, 0)
-        take_half(0, 1, 0, w_anti)
-        z_in(1, 0)
-        z_far(1, 1)
-        take_half(0, 1, 1, w_anti)
-
-    end_y(0, 1, 1)
-
-    @when_not
-    def _():
-        mid_x(0, 0)
-        end_x(0, 0)
-
-    end_y(0, 0, 1)
-
-    @when_not
-    def _():
-        relay_x(0, 1)
-
-    end_y(0, 1, 0)
-
-    @when_not
-    def _():
-        mid_x(0, 1)
-        wait_sib(0, 1)
-        wait_sib(0, 0)
-
-    away0()
-
-    @when_master
-    def _():
-        wait_sib(0, 1)
-        take_half(1, 1, 1, w_in)
-
-
-    @when_not
-    def _():
         take_half(1, 0, 0, w_far)
         end_x(0, 1)
-        take_half(1, 1, 0, w_anti)
-
-    own0()
-
-    @when_master
-    def _():
-        z_anti(1, 1)
-        relay_x(1, 1)
-        relay_x(1, 0)
-
-
-    @when_not
-    def _():
+        pass_on(1, 1)
         take_half(1, 0, 1, w_far)
-
+        pass_on(1, 0)
+
+    own0(1 - zh)
     gate()
 
     @when_master
     def _():
-        mid_x(1, 0)
-
-    relay_y(1, 0, 0)
-
-    @when_master
-    def _():
-        end_x(1, 0)
-
-
-    @when_not
-    def _():
-        relay_x(1, 0)
-
-    rim()
-
-    @when_master
-    def _():
-        mid_x(1, 1)
-
-    far_y(1, 0)
-    relay_y(1, 1, 0)
-
-    @when_master
-    def _():
-        end_x(1, 1)
-
-
-    @when_not
-    def _():
-        take_half(1, 1, 1, w_anti)
-
-    far_y(1, 1)
-
-    @when_not
-    def _():
-        relay_x(1, 1)
-
-    relay_y(1, 0, 1)
-
-    @when_not
-    def _():
-        end_x(1, 0)
-
-    end_y(1, 0, 0)
-
-    @when_not
-    def _():
-        mid_x(1, 0)
-
-    wait_sib(1, 1)
-
-    @when_not
-    def _():
+        far_y(1, 0)
         mid_x(1, 1)
         end_x(1, 1)
 
-    wait_sib(1, 0)
-    end_y(1, 1, 0)
+    rim()
+
+    @when_master
+    def _():
+        relay_y(1, 0, 0)
+        relay_y(1, 1, 0)
+        far_y(1, 1)
+        relay_y(1, 0, 1)
+        end_y(1, 0, 0)
+        relay_y(1, 2, 0)
+        relay_y(1, 1, 1)
+        end_y(1, 2, 0)
+        end_y(1, 1, 0)
+        wait_sib(1, 0)
+        far_y(1, 2)
+        wait_sib(1, 1)
+
+
+    @when_not
+    def _():
+        take_half(1, 1, 0, w_anti)
+        relay_y(1, 0, 0)
+        relay_x(1, 0)
+        take_half(1, 1, 1, w_anti)
+        relay_y(1, 1, 0)
+        relay_y(1, 2, 0)
+        far_y(1, 0)
+        end_x(1, 0)
+        relay_x(1, 1)
+        mid_x(1, 1)
+        end_y(1, 1, 0)
+        end_y(1, 0, 0)
+        far_y(1, 1)
+        mid_x(1, 0)
+        relay_y(1, 0, 1)
+        wait_sib(1, 0)
+        relay_y(1, 1, 1)
+        far_y(1, 2)
+        end_x(1, 1)
+        wait_sib(1, 1)
+
+    near2(0)
+
+    @when_master
+    def _():
+        end_y(1, 0, 1)
+
+
+    @when_not
+    def _():
+        end_y(1, 2, 0)
+
     near2(1)
-    near2(0)
-    relay_y(1, 1, 1)
-    end_y(1, 0, 1)
+
+    @when_not
+    def _():
+        end_y(1, 0, 1)
+
     far2(0)
-    end_y(1, 1, 1)
+
+    @when_master
+    def _():
+        end_y(1, 1, 1)
+        relay_y(1, 2, 1)
+
+
+    @when_not
+    def _():
+        end_y(1, 1, 1)
+
     far2(1)
+
+    @when_not
+    def _():
+        relay_y(1, 2, 1)
+
+    near2(2)
+
+    @when_master
+    def _():
+        end_y(1, 2, 1)
+
+
+    @when_not
+    def _():
+        end_y(1, 2, 1)
+
+    far2(2)
+    result(0)
+    result(2)
     result(1)
-    result(0)
 
     def last(only):
         for name, roles in sent.items():
@@ -615,7 +610,7 @@
         last("nm")
 
 
-COPIES = 128
+COPIES = 144
 
 
 def on_device(tokens, value_weight, key_gate, query_gate, conv_filter, out_weight):
@@ -628,8 +623,8 @@
         in_specs=[hbm, hbm, hbm, hbm, vmem, hbm],
         out_specs=vmem,
         scratch_shapes=[
-            pltpu.VMEM((16, WIDTH, WIDTH), bf16),
-            pltpu.VMEM((16, WIDTH, WIDTH), bf16),
+            pltpu.VMEM((17, WIDTH, WIDTH), bf16),
+            pltpu.VMEM((17, WIDTH, WIDTH), bf16),
             pltpu.VMEM((8, ROWS, WIDTH), bf16),
             pltpu.VMEM((8, ROWS, WIDTH), bf16),
             pltpu.VMEM((WIDTH // GROUP * TAPS, 2 * TAPS), bf16),

time: 134 us -> 130 us (0.970)
  the two profiles are of different devices: /device:TPU:69 before, /device:TPU:1 now
where the time goes in v4:
time: 130 us; the launch traced here: 128 us
  Pallas kernels  126 us (97%)
  local copies, waits for them, and re-layouts  1.77 us (1%)
    pallas_call x1, Pallas kernels, on_device(): pl.pallas_call(kernel, out_shape=jax.ShapeDtypeStruct((ROWS, WIDTH), bf16...  126 us

profile of v4, /device:TPU:1, one launch (start us, length us, event | category | flops | bytes accessed | tf_op | source)
XLA Modules:
  0.0 128.1 jit_solution(3856807123149558602)
XLA Ops:
  0.0 126.3 %hyena_block.1 = bf16[384,512]{1,0:T(8,128)(2,1)} custom-call(bf16[384,512]{1,0:T(8,128)(2,1)} %tok_hbm.1, bf16[512,512]{1,0:T(8,128)(2,1)} %wv_hbm.1, bf16[384,512]{1,0:T(8,128)(2,1)} %key_hbm.1, bf16[384,512]{1,0:T(8,128)(2,1)} %query_hbm.1, f32[32,128]{1,0:T(8,128)} %filt_ref.1, bf16[512,512]{1,0:T(8,128)(2,1)} %wo_hbm.1), custom_call_target="tpu_custom_call" | custom-call | flops 6442450944 | bytes 3000000 | tf_op jit(solution)/shard_map/hyena_block/pallas_call | solution.py:620
  126.3 1.8 %copy.8 = bf16[384,512]{1,0:T(8,128)(2,1)} copy(bf16[384,512]{1,0:T(8,128)(2,1)} %hyena_block.1) | data formatting | bytes 786432

commit v5 on v4

--- a/solution.py
+++ b/solution.py
@@ -262,6 +262,15 @@
     @when_not
     def _():
         z_far(0, 0)
+
+
+    @when_master
+    def _():
+        send_y(0, 0, 0)
+
+
+    @when_not
+    def _():
         z_in(0, 0)
 
 
@@ -399,71 +408,71 @@
     def _():
         relay_x(0, 0)
         take_half(0, 1, 0, w_in)
+        z_pre(0, 0)
         x_master(1)
-        z_pre(0, 0)
-        send_y(0, 0, 0)
         relay_y(0, 0, 0)
         take_half(0, 1, 1, w_in)
         t_z(0)
-        relay_x(0, 1)
         z_pre(0, 1)
         t_z(1)
         relay_x(1, 0)
-        end_y(0, 0, 0)
+        relay_x(0, 1)
+        mid_x(0, 1)
+        mid_x(1, 0)
+        end_x(0, 0)
+        end_x(0, 1)
         z_pre(1, 0)
+        mid_x(0, 0)
+        far_y(0, 1)
         far_y(0, 0)
-        end_x(0, 0)
-        far_y(0, 1)
-        mid_x(0, 1)
-        end_x(0, 1)
         z_pre(1, 1)
         relay_y(0, 1, 1)
-        mid_x(0, 0)
         send_y(0, 1, 0)
+        take_half(1, 1, 0, w_in)
         relay_y(0, 0, 1)
+        relay_y(0, 1, 0)
+        take_half(1, 1, 1, w_in)
+        end_y(0, 0, 0)
         end_y(0, 1, 1)
-        take_half(1, 1, 0, w_in)
-        mid_x(1, 0)
-        relay_y(0, 1, 0)
         end_y(0, 0, 1)
-        end_y(0, 1, 0)
-        take_half(1, 1, 1, w_in)
         end_x(1, 0)
         wait_sib(0, 0)
-
-
-    @when_not
-    def _():
+        end_y(0, 1, 0)
+
+
+    @when_not
+    def _():
+        send_y(0, 0, 0)
+        t_z(0)
+        send_y(0, 1, 0)
+        relay_y(0, 0, 0)
         z_far(0, 1)
-        t_z(0)
-        send_y(0, 0, 0)
-        relay_y(0, 0, 0)
         z_in(0, 1)
         t_z(1)
         end_y(0, 0, 0)
         z_in(1, 1)
+        take_half(0, 0, 0, w_far)
         far_y(0, 1)
-        take_half(0, 0, 0, w_far)
-        send_y(0, 1, 0)
+        pass_on(0, 0)
         far_y(0, 0)
-        pass_on(0, 0)
+        relay_y(0, 1, 1)
         pass_on(0, 1)
+        z_far(1, 0)
         take_half(0, 0, 1, w_far)
-        relay_y(0, 1, 1)
-        z_far(1, 0)
         relay_y(0, 0, 1)
         relay_x(0, 0)
-        mid_x(0, 0)
         end_y(0, 1, 1)
         relay_y(0, 1, 0)
+        z_far(1, 1)
         take_half(0, 1, 0, w_anti)
         end_x(0, 0)
+        end_y(0, 1, 0)
         end_y(0, 0, 1)
+        mid_x(0, 0)
+        wait_sib(0, 1)
         z_in(1, 0)
-        wait_sib(0, 1)
-        end_y(0, 1, 0)
+        pass_on(1, 0)
         take_half(0, 1, 1, w_anti)
-        z_far(1, 1)
 
     away0()
 
@@ -491,57 +500,56 @@
         end_x(0, 1)
         pass_on(1, 1)
         take_half(1, 0, 1, w_far)
-        pass_on(1, 0)
 
     own0(1 - zh)
     gate()
 
     @when_master
     def _():
+        end_x(1, 1)
         far_y(1, 0)
-        mid_x(1, 1)
-        end_x(1, 1)
-
-    rim()
-
-    @when_master
-    def _():
         relay_y(1, 0, 0)
         relay_y(1, 1, 0)
+
+    rim()
+
+    @when_master
+    def _():
+        mid_x(1, 1)
         far_y(1, 1)
-        relay_y(1, 0, 1)
         end_y(1, 0, 0)
         relay_y(1, 2, 0)
+        relay_y(1, 0, 1)
+        end_y(1, 2, 0)
+        far_y(1, 2)
+        wait_sib(1, 0)
         relay_y(1, 1, 1)
-        end_y(1, 2, 0)
         end_y(1, 1, 0)
-        wait_sib(1, 0)
+        wait_sib(1, 1)
+
+
+    @when_not
+    def _():
+        relay_x(1, 0)
+        take_half(1, 1, 0, w_anti)
+        relay_y(1, 0, 0)
+        relay_y(1, 2, 0)
+        take_half(1, 1, 1, w_anti)
+        relay_y(1, 1, 0)
+        end_x(1, 0)
+        far_y(1, 0)
+        relay_x(1, 1)
+        end_y(1, 1, 0)
+        mid_x(1, 1)
+        far_y(1, 1)
+        end_y(1, 0, 0)
+        mid_x(1, 0)
+        relay_y(1, 0, 1)
+        relay_y(1, 1, 1)
+        end_x(1, 1)
         far_y(1, 2)
         wait_sib(1, 1)
-
-
-    @when_not
-    def _():
-        take_half(1, 1, 0, w_anti)
-        relay_y(1, 0, 0)
-        relay_x(1, 0)
-        take_half(1, 1, 1, w_anti)
-        relay_y(1, 1, 0)
-        relay_y(1, 2, 0)
-        far_y(1, 0)
-        end_x(1, 0)
-        relay_x(1, 1)
-        mid_x(1, 1)
-        end_y(1, 1, 0)
-        end_y(1, 0, 0)
-        far_y(1, 1)
-        mid_x(1, 0)
-        relay_y(1, 0, 1)
         wait_sib(1, 0)
-        relay_y(1, 1, 1)
-        far_y(1, 2)
-        end_x(1, 1)
-        wait_sib(1, 1)
 
     near2(0)
 
@@ -552,15 +560,10 @@
 
     @when_not
     def _():
-        end_y(1, 2, 0)
-
+        end_y(1, 0, 1)
+
+    far2(0)
     near2(1)
-
-    @when_not
-    def _():
-        end_y(1, 0, 1)
-
-    far2(0)
 
     @when_master
     def _():
@@ -576,6 +579,7 @@
 
     @when_not
     def _():
+        end_y(1, 2, 0)
         relay_y(1, 2, 1)
 
     near2(2)
@@ -590,8 +594,8 @@
         end_y(1, 2, 1)
 
     far2(2)
+    result(2)
     result(0)
-    result(2)
     result(1)
 
     def last(only):

time: 130 us -> 133 us (1.023)
  Pallas kernels: 126 us -> 131 us
    pallas_call x1, Pallas kernels: 126 us -> 131 us  [on_device(): pl.pallas_call(kernel, out_shape=jax.ShapeDtypeStruct((ROWS, WIDTH), bf16...]
where the time goes in v5:
time: 133 us; the launch traced here: 132 us
  Pallas kernels  131 us (98%)
  local copies, waits for them, and re-layouts  1.77 us (1%)
    pallas_call x1, Pallas kernels, on_device(): pl.pallas_call(kernel, out_shape=jax.ShapeDtypeStruct((ROWS, WIDTH), bf16...  131 us

profile of v5, /device:TPU:1, one launch (start us, length us, event | category | flops | bytes accessed | tf_op | source)
XLA Modules:
  0.0 132.3 jit_solution(16972930777173189301)
XLA Ops:
  0.0 130.6 %hyena_block.1 = bf16[384,512]{1,0:T(8,128)(2,1)} custom-call(bf16[384,512]{1,0:T(8,128)(2,1)} %tok_hbm.1, bf16[512,512]{1,0:T(8,128)(2,1)} %wv_hbm.1, bf16[384,512]{1,0:T(8,128)(2,1)} %key_hbm.1, bf16[384,512]{1,0:T(8,128)(2,1)} %query_hbm.1, f32[32,128]{1,0:T(8,128)} %filt_ref.1, bf16[512,512]{1,0:T(8,128)(2,1)} %wo_hbm.1), custom_call_target="tpu_custom_call" | custom-call | flops 6442450944 | bytes 3000000 | tf_op jit(solution)/shard_map/hyena_block/pallas_call | solution.py:624
  130.6 1.8 %copy.8 = bf16[384,512]{1,0:T(8,128)(2,1)} copy(bf16[384,512]{1,0:T(8,128)(2,1)} %hyena_block.1) | data formatting | bytes 786432

commit v6 on v4

--- a/solution.py
+++ b/solution.py
@@ -15,7 +15,6 @@
 HALF = WIDTH // 2
 RELAY = 16
 CHUNKS = (((0, 192), (192, 192)), ((128, 128), (256, 128), (0, 128)))
-WHOLE = (0, ROWS)
 
 
 class Names:
@@ -174,7 +173,7 @@
         return copy(("tz", q, ch_), src, ref, dev_z2)
 
     def partial(q, ch_):
-        rows = pl.ds(*(WHOLE if q == 0 else CHUNKS[1][ch_]))
+        rows = pl.ds(*CHUNKS[q][ch_])
         return copy(("c", q, ch_), part_out.at[q, rows], part_in.at[q, rows], dev_z1)
 
     def halo():
@@ -346,10 +345,12 @@
             own_w(0).wait()
             own_w(1).wait()
 
-        for zz in range(2):
-            multiply(0, acc_away, every, away, zz)
-        part_out[0] = acc_away[...].astype(jnp.bfloat16)
-        partial(0, 0).start()
+        for ch_ in range(2):
+            rows = pl.ds(*CHUNKS[0][ch_])
+            for zz in range(2):
+                multiply(0, acc_away, rows, away, zz)
+            part_out[0, rows] = acc_away[rows].astype(jnp.bfloat16)
+            partial(0, ch_).start()
         acc_away[...] = jnp.zeros_like(acc_away)
 
     def own0(zz):
@@ -359,11 +360,13 @@
         own_key.wait()
         own_query.wait()
         partial(0, 0).wait_recv()
+        partial(0, 1).wait_recv()
         values = (acc_own[...] + part_in[0].astype(jnp.float32)).astype(jnp.bfloat16)
         ext[pl.ds(TAPS, ROWS), :] = (values.astype(jnp.float32) * key[...].astype(jnp.float32)).astype(jnp.bfloat16)
         halo().start()
-        convolve((1, 2))
+        convolve((1,))
         send_shaped(0)
+        convolve((2,))
         send_shaped(1)
         acc_own[...] = jnp.zeros_like(acc_own)
 

time: 130 us -> 131 us (level)
  Pallas kernels: 126 us -> 128 us
    pallas_call x1, Pallas kernels: 126 us -> 128 us  [on_device(): pl.pallas_call(kernel, out_shape=jax.ShapeDtypeStruct((ROWS, WIDTH), bf16...]
where the time goes in v6:
time: 131 us; the launch traced here: 130 us
  Pallas kernels  128 us (98%)
  local copies, waits for them, and re-layouts  1.77 us (1%)
    pallas_call x1, Pallas kernels, on_device(): pl.pallas_call(kernel, out_shape=jax.ShapeDtypeStruct((ROWS, WIDTH), bf16...  128 us

profile of v6, /device:TPU:1, one launch (start us, length us, event | category | flops | bytes accessed | tf_op | source)
XLA Modules:
  0.0 129.9 jit_solution(9634089006213236128)
XLA Ops:
  0.0 128.1 %hyena_block.1 = bf16[384,512]{1,0:T(8,128)(2,1)} custom-call(bf16[384,512]{1,0:T(8,128)(2,1)} %tok_hbm.1, bf16[512,512]{1,0:T(8,128)(2,1)} %wv_hbm.1, bf16[384,512]{1,0:T(8,128)(2,1)} %key_hbm.1, bf16[384,512]{1,0:T(8,128)(2,1)} %query_hbm.1, f32[32,128]{1,0:T(8,128)} %filt_ref.1, bf16[512,512]{1,0:T(8,128)(2,1)} %wo_hbm.1), custom_call_target="tpu_custom_call" | custom-call | flops 6442450944 | bytes 3000000 | tf_op jit(solution)/shard_map/hyena_block/pallas_call | solution.py:623
  128.1 1.8 %copy.8 = bf16[384,512]{1,0:T(8,128)(2,1)} copy(bf16[384,512]{1,0:T(8,128)(2,1)} %hyena_block.1) | data formatting | bytes 786432
